TPU v7x, 256 devices: a whole 4x4x8 slice. The times are simulated.
256 devices in a mesh: seq: 64 (over z_lo, x, y), fold: 4 (over z_hi, core).
Axes of the slice: x: 4, y: 4, z: 8 (z_hi: 2, z_lo: 4; z = z_hi * 4 + z_lo), core: 2. Of those that a mesh axis runs over, the one named last changes fastest.
Arguments:
- query: bfloat16 [65536, 1024], P(('seq', 'fold')), may hold values from -6 to 6
- keys: bfloat16 [65536, 128], P(('seq', 'fold')), may hold values from -6 to 6
- values: bfloat16 [65536, 128], P(('seq', 'fold')), may hold values from -6 to 6
- grad_out: bfloat16 [65536, 1024], P(('seq', 'fold')), may hold values from -6 to 6
- head_bias: float32 [8], replicated, may hold values from -7 to -4
- doc_ids: int32 [65536], P(('seq', 'fold')), may hold values from 0 to 255, never falling along the last dimension, each value on 1 to 2048 neighbouring positions
Outputs:
- grad_query: bfloat16 [65536, 1024], P(('seq', 'fold'))
- grad_keys: bfloat16 [65536, 128], P(('seq', 'fold'))
- grad_values: bfloat16 [65536, 128], P(('seq', 'fold'))
Inputs may be any that keep to these rules, and one draw needn't show every extreme that they name: `doc_ids`: ids never fall along the sequence; every document has 1 to 2048 tokens, and one has exactly 2048.
All inputs are finite; a program needn't handle non-finite values.
Results may differ from a plain program's by a relative error of at most 0.005.
Values may be sent and summed in bfloat16 or wider, within the bound.
A program may use at most 128 MiB of HBM per device.

v0:
```python
import functools
import math

import jax
import jax.numpy as jnp
from jax import lax
from jax.experimental import pallas as pl
from jax.experimental.pallas import tpu as pltpu
from jax.sharding import PartitionSpec as P

MAXDOC = 2048
MESH = pl.DeviceIdType.MESH
LOG2E = math.log2(math.e)
F32 = jnp.float32
BF16 = jnp.bfloat16


def dot_nt(a, b):
    return lax.dot_general(a, b, (((1,), (1,)), ((), ())), preferred_element_type=F32)


def dot_nn(a, b):
    return jnp.dot(a, b, preferred_element_type=F32)


def kernel(
    seq, fold, rows, dh, heads,
    bias_ref, ids_ref, query_ref, keys_ref, values_ref, grad_ref,
    out_query_ref, out_key_ref, out_value_ref,
    q_nat, q_tra, do_nat, do_tra, dom_nat, dom_tra, kv_own,
    blocks, sib_blocks, acc, own_part, part_d, part_o, sib_part, ret_out, ret_in,
    load_sem, fwd_send, fwd_recv, sib_send, sib_recv, sibp_send, sibp_recv, ret_send, ret_recv,
):
    peers = seq * fold
    me = lax.axis_index("seq") * fold + lax.axis_index("fold")
    odd = lax.rem(me, 2)
    hops = MAXDOC // rows // 2
    factor = 1.0 / math.sqrt(dh)

    def device(index):
        index = lax.rem(index + peers, peers)
        return (index // fold, lax.rem(index, fold))

    sibling = device(me + 1 - 2 * odd)

    barrier = pltpu.get_barrier_semaphore()
    for hop in range(1, hops + 1):
        for sign in (1, -1):
            pl.semaphore_signal(
                barrier, inc=1, device_id=device(me + sign * 2 * hop), device_id_type=MESH
            )
    pl.semaphore_signal(barrier, inc=1, device_id=sibling, device_id_type=MESH)

    cols = [pl.ds(h * dh, dh) for h in range(heads)]
    loads = [
        pltpu.make_async_copy(keys_ref, kv_own.at[0], load_sem.at[0]),
        pltpu.make_async_copy(values_ref, kv_own.at[1], load_sem.at[1]),
        pltpu.make_async_copy(query_ref, q_nat, load_sem.at[2]),
        pltpu.make_async_copy(grad_ref, do_nat, load_sem.at[3]),
    ]
    for load in loads:
        load.start()

    ids_row = ids_ref[...].astype(F32).reshape(1, rows)
    first = ids_row[:, 0:1]
    last = ids_row[:, rows - 1 : rows]
    ids_u = jnp.broadcast_to(ids_row, (rows, rows))
    ids_t = ids_u.T
    col_first = (ids_t[:, :dh] == first).astype(BF16)
    col_last = (ids_t[:, :dh] == last).astype(BF16)
    row_first = (ids_row == first).astype(BF16)
    row_last = (ids_row == last).astype(F32)

    def fwd(m):
        return pltpu.make_async_remote_copy(
            blocks.at[0], blocks.at[m], fwd_send.at[m - 1], fwd_recv.at[m - 1],
            device_id=device(me + 2 * m), device_id_type=MESH,
        )

    def to_sib(m):
        slot = m - odd
        return pltpu.make_async_remote_copy(
            blocks.at[m], sib_blocks.at[slot], sib_send.at[slot], sib_recv.at[slot],
            device_id=sibling, device_id_type=MESH,
        )

    def part_to_sib(slot):
        return pltpu.make_async_remote_copy(
            part_o.at[slot], sib_part.at[slot], sibp_send.at[slot], sibp_recv.at[slot],
            device_id=sibling, device_id_type=MESH,
        )

    def ret(m):
        return pltpu.make_async_remote_copy(
            ret_out.at[m - 1], ret_in.at[m - 1], ret_send.at[m - 1], ret_recv.at[m - 1],
            device_id=device(me - 2 * m), device_id_type=MESH,
        )

    loads[0].wait()
    loads[1].wait()
    blocks[0, pl.ds(0, rows)] = kv_own[0]
    blocks[0, pl.ds(rows, rows)] = kv_own[1] * col_last
    blocks[0, pl.ds(2 * rows, 16)] = jnp.broadcast_to(last, (16, dh)).astype(BF16)

    pl.semaphore_wait(barrier, 4 * hops // 2 + 1)
    for m in (2, 1, 4, 3):
        fwd(m).start()

    @pl.when(odd == 0)
    def _():
        to_sib(0).start()

    loads[2].wait()
    loads[3].wait()
    for h in range(heads):
        q_tra[cols[h], :] = q_nat[:, cols[h]].T
        do_tra[cols[h], :] = do_nat[:, cols[h]].T
    for h in range(heads):
        dom_nat[:, cols[h]] = do_nat[:, cols[h]] * col_first
        dom_tra[cols[h], :] = do_tra[cols[h], :] * row_first

    def block(k, v, g_nat, g_tra, mask, fresh):
        def scores(h):
            return dot_nt(q_nat[:, cols[h]], k), dot_nt(g_nat[:, cols[h]], v)

        grad_k = jnp.zeros((dh, rows), F32)
        grad_v = jnp.zeros((dh, rows), F32)
        ahead = scores(0)
        for h in range(heads):
            s, dp = ahead
            if h + 1 < heads:
                ahead = scores(h + 1)
            grow = jnp.exp2(s * (-factor * LOG2E) + bias_ref[h] * (-LOG2E))
            p = 1.0 / (1.0 + grow)
            if mask is not None:
                p = p * mask
            ds = (dp * (p * (1.0 - p))).astype(BF16)
            p = p.astype(BF16)
            if fresh:
                acc[:, cols[h]] = dot_nn(ds, k)
            else:
                acc[:, cols[h]] += dot_nn(ds, k)
            grad_v = grad_v + dot_nn(g_tra[cols[h], :], p)
            grad_k = grad_k + dot_nn(q_tra[cols[h], :], ds)
        return grad_k, grad_v

    iota_t = lax.broadcasted_iota(jnp.int32, (rows, rows), 0)
    iota_u = lax.broadcasted_iota(jnp.int32, (rows, rows), 1)
    mask = ((ids_t == ids_u) & (iota_u <= iota_t)).astype(F32)
    grad_k, grad_v = block(kv_own[0], kv_own[1], do_nat, do_tra, mask, True)
    own_part[pl.ds(0, dh)] = grad_k
    own_part[pl.ds(dh, dh)] = grad_v

    def arrived(m):
        fwd(m).wait_recv()

        @pl.when(m - odd < hops)
        def _():
            to_sib(m).start()

    def far_block(ref, part):
        gate = (ref[pl.ds(2 * rows, 16)][0:1].astype(F32) == first).astype(F32)
        k = ref[pl.ds(0, rows)]
        v = ref[pl.ds(rows, rows)] * gate.astype(BF16)
        grad_k, grad_v = block(k, v, dom_nat, dom_tra, None, False)
        part[pl.ds(0, dh)] = grad_k
        part[pl.ds(dh, dh)] = grad_v * jnp.concatenate([gate] * (rows // dh), axis=1)

    def order(step):
        return 2 * step + 2 - 5 * (step // 2)

    arrived(order(0))

    def body(step, carry):
        m = order(step)
        slot = lax.rem(m - 1 + odd, hops)
        to_sib(slot + odd).wait_recv()
        far_block(sib_blocks.at[slot], part_o.at[slot])
        part_to_sib(slot).start()

        @pl.when(step + 1 < hops)
        def _():
            arrived(order(step + 1))

        far_block(blocks.at[m], part_d)
        back = m - odd

        @pl.when(back < hops)
        def _():
            part_to_sib(back).wait_recv()
            ret_out[m - 1] = (part_d[...] + sib_part[back]).astype(BF16)

        @pl.when(back >= hops)
        def _():
            ret_out[m - 1] = part_d[...].astype(BF16)

        ret(m).start()
        return carry

    lax.fori_loop(0, hops, body, 0)

    out_query_ref[...] = (acc[...] * factor).astype(BF16)

    @pl.when(odd == 0)
    def _():
        part_to_sib(0).wait_recv()
        own_part[...] = own_part[...] + sib_part[0] * row_last

    total = own_part[...]
    for m in range(1, hops + 1):
        ret(m).wait_recv()
        total = total + ret_in[m - 1].astype(F32) * row_last
    out_key_ref[...] = (total[:dh] * factor).T.astype(BF16)
    out_value_ref[...] = total[dh:].T.astype(BF16)

    for m in range(1, hops + 1):
        fwd(m).wait_send()
        ret(m).wait_send()
        part_to_sib(m - 1).wait_send()
    for slot in range(hops):
        to_sib(slot + odd).wait_send()


def solution(mesh):
    seq, fold = mesh.shape["seq"], mesh.shape["fold"]

    def body(query, keys, values, grad_out, head_bias, doc_ids):
        rows, dh = keys.shape
        heads = query.shape[1] // dh
        hops = MAXDOC // rows // 2
        wide = heads * dh
        block = 2 * rows + 16
        vmem = pl.BlockSpec(memory_space=pltpu.VMEM)
        hbm = pl.BlockSpec(memory_space=pl.ANY)
        dma = pltpu.SemaphoreType.DMA
        return pl.pallas_call(
            functools.partial(kernel, seq, fold, rows, dh, heads),
            out_shape=(
                jax.ShapeDtypeStruct((rows, wide), BF16),
                jax.ShapeDtypeStruct((rows, dh), BF16),
                jax.ShapeDtypeStruct((rows, dh), BF16),
            ),
            in_specs=[pl.BlockSpec(memory_space=pltpu.SMEM), vmem, hbm, hbm, hbm, hbm],
            out_specs=(vmem, vmem, vmem),
            scratch_shapes=[
                pltpu.VMEM((rows, wide), BF16),
                pltpu.VMEM((wide, rows), BF16),
                pltpu.VMEM((rows, wide), BF16),
                pltpu.VMEM((wide, rows), BF16),
                pltpu.VMEM((rows, wide), BF16),
                pltpu.VMEM((wide, rows), BF16),
                pltpu.VMEM((2, rows, dh), BF16),
                pltpu.VMEM((hops + 1, block, dh), BF16),
                pltpu.VMEM((hops, block, dh), BF16),
                pltpu.VMEM((rows, wide), F32),
                pltpu.VMEM((2 * dh, rows), F32),
                pltpu.VMEM((2 * dh, rows), F32),
                pltpu.VMEM((hops, 2 * dh, rows), F32),
                pltpu.VMEM((hops, 2 * dh, rows), F32),
                pltpu.VMEM((hops, 2 * dh, rows), BF16),
                pltpu.VMEM((hops, 2 * dh, rows), BF16),
                dma((4,)),
                dma((hops,)), dma((hops,)),
                dma((hops,)), dma((hops,)),
                dma((hops,)), dma((hops,)),
                dma((hops,)), dma((hops,)),
            ],
            compiler_params=pltpu.CompilerParams(
                collective_id=0, has_side_effects=True, vmem_limit_bytes=56 << 20
            ),
        )(head_bias, doc_ids, query, keys, values, grad_out)

    split = P(("seq", "fold"), None)
    return jax.shard_map(
        body,
        mesh=mesh,
        in_specs=(split, split, split, split, P(), P(("seq", "fold"))),
        out_specs=(split, split, split),
        check_vma=False,
    )
```

profile of v0, /device:TPU:1, one launch (start us, length us, event | category | flops | bytes accessed | tf_op | source)
XLA Modules:
  0.0 61.0 jit_solution(8608258448889877923)
XLA Ops:
  0.6 56.9 %shard_map.85 = (bf16[256,1024]{1,0:T(8,128)(2,1)}, bf16[256,128]{1,0:T(8,128)(2,1)}, bf16[256,128]{1,0:T(8,128)(2,1)}) custom-call(f32[8]{0:T(128)} %bias_ref.1, s32[256]{0:T(256)} %ids_ref.1, bf16[256,1024]{1,0:T(8,128)(2,1)} %query_ref.1, bf16[256,128]{1,0:T(8,128)(2,1)} %keys_ref.1, bf16[256,128]{1,0:T(8,128)(2,1)} %values_ref.1, bf16[256,1024]{1,0:T(8,128)(2,1)} %grad_ref.1), custom_call_target="tpu_custom_call" | custom-call | tf_op jit(solution)/shard_map/pallas_call | solution.py:236
  57.6 0.0 copy-start.1
  57.6 1.9 %copy.12 = bf16[256,1024]{1,0:T(8,128)(2,1)} copy(bf16[256,1024]{1,0:T(8,128)(2,1)} %get-tuple-element.6) | data formatting | bytes 1048576
  59.5 0.0 copy-done.1
  59.5 0.0 copy-start
  59.5 0.6 %copy.13 = bf16[256,128]{1,0:T(8,128)(2,1)} copy(bf16[256,128]{1,0:T(8,128)(2,1)S(1)} %copy-done.1) | data formatting | bytes 131072
  60.1 0.2 copy-done
  60.4 0.6 %copy.14 = bf16[256,128]{1,0:T(8,128)(2,1)} copy(bf16[256,128]{1,0:T(8,128)(2,1)S(1)} %copy-done) | data formatting | bytes 131072
Async XLA Ops:
  57.6 1.9 %copy-start.1 = (bf16[256,128]{1,0:T(8,128)(2,1)S(1)}, bf16[256,128]{1,0:T(8,128)(2,1)}, u32[]{:S(2)}) copy-start(bf16[256,128]{1,0:T(8,128)(2,1)} %get-tuple-element.7) | copy-start | bytes 196612
  59.5 0.9 %copy-start = (bf16[256,128]{1,0:T(8,128)(2,1)S(1)}, bf16[256,128]{1,0:T(8,128)(2,1)}, u32[]{:S(2)}) copy-start(bf16[256,128]{1,0:T(8,128)(2,1)} %get-tuple-element.8) | copy-start | bytes 196612
where the time goes:
time: 61.2 us; the launch traced here: 61 us
  Pallas kernels  56.9 us (93%)
  local copies, waits for them, and re-layouts  3.4 us (6%)
  between operations  0.65 us (1%)
    pallas_call x1, Pallas kernels, body(): pl.pallas_call(functools.partial(kernel, seq, fold, rows, dh, heads), out...  56.9 us
    unnamed x7, local copies, waits for them, and re-layouts  3.4 us

commit v1 on v0

v1 whole, which is shorter than its diff:
```python
import functools
import math

import jax
import jax.numpy as jnp
from jax import lax
from jax.experimental import pallas as pl
from jax.experimental.pallas import tpu as pltpu
from jax.sharding import PartitionSpec as P

MAXDOC = 2048
MESH = pl.DeviceIdType.MESH
LOG2E = math.log2(math.e)
F32 = jnp.float32
BF16 = jnp.bfloat16


def dot_nt(a, b):
    return lax.dot_general(a, b, (((1,), (1,)), ((), ())), preferred_element_type=F32)


def dot_nn(a, b):
    return jnp.dot(a, b, preferred_element_type=F32)


def kernel(
    seq, fold, rows, dh, heads,
    bias_ref, ids_ref, query_ref, keys_ref, values_ref, grad_ref,
    out_query_ref, out_key_ref, out_value_ref,
    q_nat, q_tra, do_nat, do_tra, dom_nat, dom_tra, v_own,
    blocks, sib_blocks, acc, own_part, part_d, part_o, sib_part, ret_out, ret_in, aside_in,
    load_sem, fwd_send, fwd_recv, sib_send, sib_recv, sibp_send, sibp_recv, ret_send, ret_recv,
    aside_send, aside_recv,
):
    peers = seq * fold
    me = lax.axis_index("seq") * fold + lax.axis_index("fold")
    odd = lax.rem(me, 2)
    hops = MAXDOC // rows // 2
    factor = 1.0 / math.sqrt(dh)

    def device(index):
        index = lax.rem(index + peers, peers)
        return (index // fold, lax.rem(index, fold))

    sibling = device(me + 1 - 2 * odd)

    run = peers // 4

    def turns(index):
        return (index >= run) & (index < peers) & (lax.rem(index, run) < 2)

    turn = turns(me)
    turn_mate = turns(me - 2)
    turn_ahead = turns(me + 2)

    barrier = pltpu.get_barrier_semaphore()
    partners = jnp.int32(1)
    for hop in range(1, hops + 1):
        for far in (2 * hop, -2 * hop):
            valid = (me + far >= 0) & (me + far < peers)
            partners += valid.astype(jnp.int32)

            @pl.when(valid)
            def _():
                pl.semaphore_signal(
                    barrier, inc=1, device_id=device(me + far), device_id_type=MESH
                )

    pl.semaphore_signal(barrier, inc=1, device_id=sibling, device_id_type=MESH)

    cols = [pl.ds(h * dh, dh) for h in range(heads)]
    loads = [
        pltpu.make_async_copy(keys_ref, blocks.at[0, pl.ds(0, rows)], load_sem.at[0]),
        pltpu.make_async_copy(values_ref, v_own, load_sem.at[1]),
        pltpu.make_async_copy(query_ref, q_nat, load_sem.at[2]),
        pltpu.make_async_copy(grad_ref, do_nat, load_sem.at[3]),
    ]
    for load in loads:
        load.start()

    ids_row = ids_ref[...].astype(F32).reshape(1, rows)
    first = ids_row[:, 0:1]
    last = ids_row[:, rows - 1 : rows]
    ids_u = jnp.broadcast_to(ids_row, (rows, rows))
    ids_t = ids_u.T
    col_first = (ids_t[:, :dh] == first).astype(BF16)
    col_last = (ids_t[:, :dh] == last).astype(BF16)
    row_first = (ids_row == first).astype(BF16)
    row_last = (ids_row == last).astype(F32)

    chunks = (pl.ds(0, rows), pl.ds(rows, rows + 16))

    def push(src, dst, part, far, extra=0):
        slot = 2 * (dst - 1) + part
        return pltpu.make_async_remote_copy(
            blocks.at[src, chunks[part]], blocks.at[dst, chunks[part]],
            fwd_send.at[slot + extra], fwd_recv.at[slot],
            device_id=device(me + far), device_id_type=MESH,
        )

    def fwd(m, part):
        return push(0, m, part, 2 * m)

    def relay(m, part):
        return push(m, m + 2, part, 4)

    def sends(m):
        if m == 1:
            return (me + 2 < peers) & jnp.logical_not(turn_ahead)
        return me + 2 * m < peers

    def cross(part):
        return push(2, 1, part, -2, 2 * hops)

    def to_sib(m):
        slot = m - odd
        return pltpu.make_async_remote_copy(
            blocks.at[m], sib_blocks.at[slot], sib_send.at[slot], sib_recv.at[slot],
            device_id=sibling, device_id_type=MESH,
        )

    def part_to_sib(slot):
        return pltpu.make_async_remote_copy(
            part_o.at[slot], sib_part.at[slot], sibp_send.at[slot], sibp_recv.at[slot],
            device_id=sibling, device_id_type=MESH,
        )

    def ret(m):
        return pltpu.make_async_remote_copy(
            ret_out.at[m - 1], ret_in.at[m - 1], ret_send.at[m - 1], ret_recv.at[m - 1],
            device_id=device(me - 2 * m), device_id_type=MESH,
        )

    loads[0].wait()
    pl.semaphore_wait(barrier, partners)
    for m in (1, 2):
        pl.when(sends(m))(fwd(m, 0).start)
    loads[1].wait()
    blocks[0, pl.ds(rows, rows)] = v_own[...] * col_last
    blocks[0, pl.ds(2 * rows, 16)] = jnp.broadcast_to(last, (16, dh)).astype(BF16)
    for m in (1, 2):
        pl.when(sends(m))(fwd(m, 1).start)

    @pl.when(odd == 0)
    def _():
        to_sib(0).start()

    loads[2].wait()
    loads[3].wait()
    for h in range(heads):
        q_tra[cols[h], :] = q_nat[:, cols[h]].T
        do_tra[cols[h], :] = do_nat[:, cols[h]].T
    for h in range(heads):
        dom_nat[:, cols[h]] = do_nat[:, cols[h]] * col_first
        dom_tra[cols[h], :] = do_tra[cols[h], :] * row_first

    def block(k, v, g_nat, g_tra, mask):
        def scores(h):
            return dot_nt(q_nat[:, cols[h]], k), dot_nt(g_nat[:, cols[h]], v)

        grad_k = jnp.zeros((dh, rows), F32)
        grad_v = jnp.zeros((dh, rows), F32)
        ahead = scores(0)
        for h in range(heads):
            s, dp = ahead
            if h + 1 < heads:
                ahead = scores(h + 1)
            grow = jnp.exp2(s * (-factor * LOG2E) + bias_ref[h] * (-LOG2E))
            p = 1.0 / (1.0 + grow)
            if mask is not None:
                p = p * mask
            ds = (dp * (p * (1.0 - p))).astype(BF16)
            p = p.astype(BF16)
            acc[:, cols[h]] += dot_nn(ds, k)
            grad_v = grad_v + dot_nn(g_tra[cols[h], :], p)
            grad_k = grad_k + dot_nn(q_tra[cols[h], :], ds)
        return grad_k, grad_v

    acc[...] = jnp.zeros(acc.shape, F32)

    def own_block():
        iota_t = lax.broadcasted_iota(jnp.int32, (rows, rows), 0)
        iota_u = lax.broadcasted_iota(jnp.int32, (rows, rows), 1)
        mask = ((ids_t == ids_u) & (iota_u <= iota_t)).astype(F32)
        grad_k, grad_v = block(blocks[0, pl.ds(0, rows)], v_own[...], do_nat, do_tra, mask)
        own_part[pl.ds(0, dh)] = grad_k
        own_part[pl.ds(dh, dh)] = grad_v

    def relays(m):
        return (m <= 2) & (me >= 2 * m) & (me + 4 < peers)

    def arrived(m, part):
        pl.when(me >= 2 * m)(fwd(m, part).wait_recv)

        @pl.when(me < 2 * m)
        def _():
            blocks[m, chunks[part]] = jnp.full((rows + 16 * part, dh), -1.0, BF16)

        @pl.when(relays(m))
        def _():
            relay(m, part).start()

        @pl.when((m == 2) & turn_mate)
        def _():
            cross(part).start()

    def far_block(ref, part):
        gate = (ref[pl.ds(2 * rows, 16)][0:1].astype(F32) == first).astype(F32)
        k = ref[pl.ds(0, rows)]
        v = ref[pl.ds(rows, rows)] * gate.astype(BF16)
        grad_k, grad_v = block(k, v, dom_nat, dom_tra, None)
        part[pl.ds(0, dh)] = grad_k
        part[pl.ds(dh, dh)] = grad_v * jnp.concatenate([gate] * (rows // dh), axis=1)

    def order(step):
        return step + 2 - 2 * lax.rem(step, 2)

    def aside():
        return pltpu.make_async_remote_copy(
            ret_out.at[0], aside_in, aside_send, aside_recv,
            device_id=device(me + 2), device_id_type=MESH,
        )

    def send_back(m):
        back = m - odd

        @pl.when(back < hops)
        def _():
            part_to_sib(back).wait_recv()
            ret_out[m - 1] = (part_d[m - 1] + sib_part[back]).astype(BF16)

        @pl.when(back >= hops)
        def _():
            ret_out[m - 1] = part_d[m - 1].astype(BF16)

        @pl.when((m == 2) & turn_mate)
        def _():
            aside().wait_recv()
            ret_out[1] = (ret_out[1].astype(F32) + aside_in[...].astype(F32)).astype(BF16)

        pl.when((m == 1) & turn)(aside().start)
        pl.when((me >= 2 * m) & jnp.logical_not((m == 1) & turn))(ret(m).start)

    def body(step, carry):
        m = order(step)
        slot = lax.rem(m - 1 + odd, hops)
        pl.when(step != 1)(functools.partial(arrived, m, 0))
        arrived(m, 1)

        @pl.when(m - odd < hops)
        def _():
            to_sib(m).start()

        far_block(blocks.at[m], part_d.at[m - 1])

        @pl.when((step > 0) & jnp.logical_not((step == 1) & turn_mate))
        def _():
            send_back(order(step - 1))

        to_sib(slot + odd).wait_recv()
        far_block(sib_blocks.at[slot], part_o.at[slot])
        part_to_sib(slot).start()

        @pl.when(step == 0)
        def _():
            arrived(order(1), 0)
            own_block()

        return carry

    lax.fori_loop(0, hops, body, 0)

    out_query_ref[...] = (acc[...] * factor).astype(BF16)
    send_back(order(hops - 1))

    @pl.when(turn_mate)
    def _():
        send_back(jnp.int32(2))

    @pl.when(odd == 0)
    def _():
        part_to_sib(0).wait_recv()
        own_part[...] = own_part[...] + sib_part[0] * row_last

    for m in (2, 1, 4, 3):

        @pl.when(sends(m))
        def _():
            ret(m).wait_recv()
            own_part[...] = own_part[...] + ret_in[m - 1].astype(F32) * row_last

    out_key_ref[...] = (own_part[pl.ds(0, dh)] * factor).T.astype(BF16)
    out_value_ref[...] = own_part[pl.ds(dh, dh)].T.astype(BF16)
    for m in range(1, hops + 1):
        if m <= 2:
            for part in (0, 1):
                pl.when(sends(m))(fwd(m, part).wait_send)
                pl.when(relays(m))(relay(m, part).wait_send)
        if m == 1:
            pl.when((me >= 2) & jnp.logical_not(turn))(ret(m).wait_send)
            pl.when(turn)(aside().wait_send)
        else:
            pl.when(me >= 2 * m)(ret(m).wait_send)
        if m == 2:
            for part in (0, 1):
                pl.when(turn_mate)(cross(part).wait_send)
        part_to_sib(m - 1).wait_send()
    for slot in range(hops):
        to_sib(slot + odd).wait_send()


def hand_on(q_in, k_in, v_in, q_out, k_out, v_out, sem):
    copies = [
        pltpu.make_async_copy(src, dst, sem.at[i])
        for i, (src, dst) in enumerate(((q_in, q_out), (k_in, k_out), (v_in, v_out)))
    ]
    for copy in copies:
        copy.start()
    for copy in copies:
        copy.wait()


def solution(mesh):
    seq, fold = mesh.shape["seq"], mesh.shape["fold"]

    def body(query, keys, values, grad_out, head_bias, doc_ids):
        rows, dh = keys.shape
        heads = query.shape[1] // dh
        hops = MAXDOC // rows // 2
        wide = heads * dh
        block = 2 * rows + 16
        vmem = pl.BlockSpec(memory_space=pltpu.VMEM)
        hbm = pl.BlockSpec(memory_space=pl.ANY)
        dma = pltpu.SemaphoreType.DMA
        shapes = (
            jax.ShapeDtypeStruct((rows, wide), BF16),
            jax.ShapeDtypeStruct((rows, dh), BF16),
            jax.ShapeDtypeStruct((rows, dh), BF16),
        )
        grads = pl.pallas_call(
            functools.partial(kernel, seq, fold, rows, dh, heads),
            out_shape=tuple(pltpu.VMEM(x.shape, x.dtype) for x in shapes),
            in_specs=[pl.BlockSpec(memory_space=pltpu.SMEM), vmem, hbm, hbm, hbm, hbm],
            out_specs=(vmem, vmem, vmem),
            scratch_shapes=[
                pltpu.VMEM((rows, wide), BF16),
                pltpu.VMEM((wide, rows), BF16),
                pltpu.VMEM((rows, wide), BF16),
                pltpu.VMEM((wide, rows), BF16),
                pltpu.VMEM((rows, wide), BF16),
                pltpu.VMEM((wide, rows), BF16),
                pltpu.VMEM((rows, dh), BF16),
                pltpu.VMEM((hops + 1, block, dh), BF16),
                pltpu.VMEM((hops, block, dh), BF16),
                pltpu.VMEM((rows, wide), F32),
                pltpu.VMEM((2 * dh, rows), F32),
                pltpu.VMEM((hops, 2 * dh, rows), F32),
                pltpu.VMEM((hops, 2 * dh, rows), F32),
                pltpu.VMEM((hops, 2 * dh, rows), F32),
                pltpu.VMEM((hops, 2 * dh, rows), BF16),
                pltpu.VMEM((hops, 2 * dh, rows), BF16),
                pltpu.VMEM((2 * dh, rows), BF16),
                dma((4,)),
                dma((2 * hops + 2,)), dma((2 * hops,)),
                dma((hops,)), dma((hops,)),
                dma((hops,)), dma((hops,)),
                dma((hops,)), dma((hops,)),
                dma, dma,
            ],
            compiler_params=pltpu.CompilerParams(
                collective_id=0, has_side_effects=True, vmem_limit_bytes=58 << 20
            ),
        )(head_bias, doc_ids, query, keys, values, grad_out)
        return pl.pallas_call(
            hand_on,
            out_shape=shapes,
            in_specs=[vmem] * 3,
            out_specs=(hbm,) * 3,
            scratch_shapes=[dma((3,))],
            compiler_params=pltpu.CompilerParams(vmem_limit_bytes=1 << 20),
        )(*grads)

    split = P(("seq", "fold"), None)
    return jax.shard_map(
        body,
        mesh=mesh,
        in_specs=(split, split, split, split, P(), P(("seq", "fold"))),
        out_specs=(split, split, split),
        check_vma=False,
    )
```

time: 61.2 us -> 47 us (0.77)
  the two profiles are of different devices: /device:TPU:1 before, /device:TPU:222 now
where the time goes in v1:
time: 47 us; the launch traced here: 46.9 us
  Pallas kernels  46.2 us (98%)
  between operations  0.64 us (1%)
    pallas_call x1, Pallas kernels, body(): pl.pallas_call(functools.partial(kernel, seq, fold, rows, dh, heads), out...  45.4 us

profile of v1, /device:TPU:222, one launch (start us, length us, event | category | flops | bytes accessed | tf_op | source)
XLA Modules:
  0.0 46.9 jit_solution(10907549174711793650)
XLA Ops:
  0.6 45.4 %shard_map.85 = (bf16[256,1024]{1,0:T(8,128)(2,1)S(1)}, bf16[256,128]{1,0:T(8,128)(2,1)S(1)}, bf16[256,128]{1,0:T(8,128)(2,1)S(1)}) custom-call(f32[8]{0:T(128)} %bias_ref.1, s32[256]{0:T(256)} %ids_ref.1, bf16[256,1024]{1,0:T(8,128)(2,1)} %query_ref.1, bf16[256,128]{1,0:T(8,128)(2,1)} %keys_ref.1, bf16[256,128]{1,0:T(8,128)(2,1)} %values_ref.1, ...), custom_call_target="tpu_custom_call" | custom-call | tf_op jit(solution)/shard_map/pallas_call | solution.py:340
  46.0 0.9 %shard_map.86 = (bf16[256,1024]{1,0:T(8,128)(2,1)}, bf16[256,128]{1,0:T(8,128)(2,1)}, bf16[256,128]{1,0:T(8,128)(2,1)}) custom-call(bf16[256,1024]{1,0:T(8,128)(2,1)S(1)} %get-tuple-element.6.q_in, bf16[256,128]{1,0:T(8,128)(2,1)S(1)} %get-tuple-element.7.k_in, bf16[256,128]{1,0:T(8,128)(2,1)S(1)} %get-tuple-element.8.v_in), custom_call_target="tpu_custom_call" | custom-call | tf_op jit(solution)/shard_map/pallas_call | solution.py:374

commit v2 on v1

v2 whole, which is shorter than its diff:
```python
import functools
import math

import jax
import jax.numpy as jnp
from jax import lax
from jax.experimental import pallas as pl
from jax.experimental.pallas import tpu as pltpu
from jax.sharding import PartitionSpec as P

MAXDOC = 2048
MESH = pl.DeviceIdType.MESH
LOG2E = math.log2(math.e)
F32 = jnp.float32
BF16 = jnp.bfloat16


def dot_nt(a, b):
    return lax.dot_general(a, b, (((1,), (1,)), ((), ())), preferred_element_type=F32)


def dot_nn(a, b):
    return jnp.dot(a, b, preferred_element_type=F32)


def kernel(
    seq, fold, rows, dh, heads,
    bias_ref, ids_ref, query_ref, keys_ref, values_ref, grad_ref,
    out_query_ref, out_key_ref, out_value_ref,
    q_nat, q_tra, do_nat, do_tra, dom_nat, dom_tra, v_own,
    blocks, sib_blocks, acc, own_part, part_d, part_o, sib_part, ret_out, ret_in, aside_in,
    load_sem, fwd_send, fwd_recv, sib_send, sib_recv, sibp_send, sibp_recv, ret_send, ret_recv,
    aside_send, aside_recv,
):
    peers = seq * fold
    me = lax.axis_index("seq") * fold + lax.axis_index("fold")
    odd = lax.rem(me, 2)
    hops = MAXDOC // rows // 2
    half = rows // 2
    factor = 1.0 / math.sqrt(dh)
    run = peers // 4

    def device(index):
        index = lax.rem(index + peers, peers)
        return (index // fold, lax.rem(index, fold))

    def turns(index):
        return (index >= run) & (index < peers) & (lax.rem(index, run) < 2)

    sibling = device(me + 1 - 2 * odd)
    turn = turns(me)
    turn_mate = turns(me - 2)
    turn_ahead = turns(me + 2)

    barrier = pltpu.get_barrier_semaphore()
    partners = jnp.int32(1)
    for hop in range(1, hops + 1):
        for far in (2 * hop, -2 * hop):
            valid = (me + far >= 0) & (me + far < peers)
            partners += valid.astype(jnp.int32)

            @pl.when(valid)
            def _():
                pl.semaphore_signal(
                    barrier, inc=1, device_id=device(me + far), device_id_type=MESH
                )

    pl.semaphore_signal(barrier, inc=1, device_id=sibling, device_id_type=MESH)

    cols = [pl.ds(h * dh, dh) for h in range(heads)]
    parts = [pl.ds(c * half, half) for c in (0, 1)]
    k_rows, v_rows, id_rows = pl.ds(0, half), pl.ds(half, half), pl.ds(rows, 16)
    loads = [
        pltpu.make_async_copy(keys_ref.at[parts[0]], blocks.at[0, 0, k_rows], load_sem.at[0]),
        pltpu.make_async_copy(keys_ref.at[parts[1]], blocks.at[0, 1, k_rows], load_sem.at[1]),
        pltpu.make_async_copy(values_ref, v_own, load_sem.at[2]),
        pltpu.make_async_copy(query_ref, q_nat, load_sem.at[3]),
        pltpu.make_async_copy(grad_ref, do_nat, load_sem.at[4]),
    ]
    for load in loads:
        load.start()

    ids_row = ids_ref[...].astype(F32).reshape(1, rows)
    first = ids_row[:, 0:1]
    last = ids_row[:, rows - 1 : rows]
    ids_u = jnp.broadcast_to(ids_row, (rows, rows))
    ids_t = ids_u.T
    col_first = (ids_t[:, :dh] == first).astype(BF16)
    col_last = (ids_t[:, :dh] == last).astype(BF16)
    row_first = (ids_row == first).astype(BF16)
    row_last = (ids_row == last).astype(F32)

    def push(src, dst, c, far, extra=0):
        slot = 2 * (dst - 1) + c
        return pltpu.make_async_remote_copy(
            blocks.at[src, c], blocks.at[dst, c],
            fwd_send.at[slot + extra], fwd_recv.at[slot],
            device_id=device(me + far), device_id_type=MESH,
        )

    def fwd(m, c):
        return push(0, m, c, 2 * m)

    def relay(m, c):
        return push(m, m + 2, c, 4)

    def cross(c):
        return push(2, 1, c, -2, 2 * hops)

    def sends(m, c):
        if m == 1 and c == 0:
            return (me + 2 < peers) & jnp.logical_not(turn_ahead)
        return me + 2 * m < peers

    def returns(m):
        if m == 1:
            return (me + 2 < peers) & jnp.logical_not(turn_ahead)
        return me + 2 * m < peers

    def relays(m):
        return (me >= 2 * m) & (me + 4 < peers)

    def to_sib(m, c):
        slot = m - odd
        return pltpu.make_async_remote_copy(
            blocks.at[m, c], sib_blocks.at[slot, c],
            sib_send.at[2 * slot + c], sib_recv.at[2 * slot + c],
            device_id=sibling, device_id_type=MESH,
        )

    def part_to_sib(slot, c):
        return pltpu.make_async_remote_copy(
            part_o.at[slot, c], sib_part.at[slot, c],
            sibp_send.at[2 * slot + c], sibp_recv.at[2 * slot + c],
            device_id=sibling, device_id_type=MESH,
        )

    def ret(m, c):
        slot = 2 * (m - 1) + c
        return pltpu.make_async_remote_copy(
            ret_out.at[m - 1, c], ret_in.at[m - 1, c], ret_send.at[slot], ret_recv.at[slot],
            device_id=device(me - 2 * m), device_id_type=MESH,
        )

    def aside(c):
        return pltpu.make_async_remote_copy(
            ret_out.at[0, c], aside_in.at[c], aside_send.at[c], aside_recv.at[c],
            device_id=device(me + 2), device_id_type=MESH,
        )

    for load in loads[:3]:
        load.wait()
    for c in (0, 1):
        blocks[0, c, v_rows] = v_own[parts[c]] * col_last[c * half : c * half + half]
        blocks[0, c, id_rows] = jnp.broadcast_to(last, (16, dh)).astype(BF16)
    pl.semaphore_wait(barrier, partners)
    for c in (0, 1):
        for m in (1, 2):
            pl.when(sends(m, c))(fwd(m, c).start)

    @pl.when(odd == 0)
    def _():
        for c in (0, 1):
            to_sib(0, c).start()

    for load in loads[3:]:
        load.wait()
    for h in range(heads):
        q_tra[cols[h], :] = q_nat[:, cols[h]].T
        do_tra[cols[h], :] = do_nat[:, cols[h]].T
    for h in range(heads):
        dom_nat[:, cols[h]] = do_nat[:, cols[h]] * col_first
        dom_tra[cols[h], :] = do_tra[cols[h], :] * row_first

    def block(k, v, g_nat, g_tra, mask):
        def scores(h):
            return dot_nt(q_nat[:, cols[h]], k), dot_nt(g_nat[:, cols[h]], v)

        grad_k = jnp.zeros((dh, rows), F32)
        grad_v = jnp.zeros((dh, rows), F32)
        ahead = scores(0)
        for h in range(heads):
            s, dp = ahead
            if h + 1 < heads:
                ahead = scores(h + 1)
            grow = jnp.exp2(s * (-factor * LOG2E) + bias_ref[h] * (-LOG2E))
            p = 1.0 / (1.0 + grow)
            if mask is not None:
                p = p * mask
            ds = (dp * (p * (1.0 - p))).astype(BF16)
            p = p.astype(BF16)
            if mask is not None:
                acc[:, cols[h]] = dot_nn(ds, k)
            else:
                acc[:, cols[h]] += dot_nn(ds, k)
            grad_v = grad_v + dot_nn(g_tra[cols[h], :], p)
            grad_k = grad_k + dot_nn(q_tra[cols[h], :], ds)
        return grad_k, grad_v

    iota_t = lax.broadcasted_iota(jnp.int32, (rows, rows), 0)
    iota_u = lax.broadcasted_iota(jnp.int32, (rows, rows), 1)
    own_mask = ((ids_t == ids_u) & (iota_u <= iota_t)).astype(F32)
    own_k = jnp.concatenate([blocks[0, c, k_rows] for c in (0, 1)], axis=0)
    grad_k, grad_v = block(own_k, v_own[...], do_nat, do_tra, own_mask)
    own_part[pl.ds(0, dh)] = grad_k
    own_part[pl.ds(dh, dh)] = grad_v

    def arrived(m, c):
        pl.when(me >= 2 * m)(fwd(m, c).wait_recv)

        @pl.when(me < 2 * m)
        def _():
            blocks[m, c] = jnp.full((rows + 16, dh), -1.0, BF16)

        if m <= 2:
            pl.when(relays(m))(relay(m, c).start)
        if m == 2 and c == 0:
            pl.when(turn_mate)(cross(c).start)
        pl.when(m - odd < hops)(to_sib(m, c).start)

    def far_blocks(m, slot, c):
        refs = (blocks.at[m, c], sib_blocks.at[slot, c])
        gates = [(ref[id_rows][0:1].astype(F32) == first).astype(F32) for ref in refs]
        k = jnp.concatenate([ref[k_rows] for ref in refs], axis=0)
        v = jnp.concatenate(
            [ref[v_rows] * gate.astype(BF16) for ref, gate in zip(refs, gates)], axis=0
        )
        grad_k, grad_v = block(k, v, dom_nat, dom_tra, None)
        grad_v = grad_v * jnp.concatenate(gates, axis=1)
        part_d[m - 1, c, pl.ds(0, dh)] = grad_k[:, :half]
        part_d[m - 1, c, pl.ds(dh, dh)] = grad_v[:, :half]
        part_o[slot, c, pl.ds(0, dh)] = grad_k[:, half:]
        part_o[slot, c, pl.ds(dh, dh)] = grad_v[:, half:]

    def send_back(m, c):
        back = m - odd

        @pl.when(back < hops)
        def _():
            part_to_sib(back, c).wait_recv()
            ret_out[m - 1, c] = (part_d[m - 1, c] + sib_part[back, c]).astype(BF16)

        @pl.when(back >= hops)
        def _():
            ret_out[m - 1, c] = part_d[m - 1, c].astype(BF16)

        if m == 2:

            @pl.when(turn_mate)
            def _():
                aside(c).wait_recv()
                ret_out[1, c] = (
                    ret_out[1, c].astype(F32) + aside_in[c].astype(F32)
                ).astype(BF16)

        if m == 1:
            pl.when(turn)(aside(c).start)
            pl.when((me >= 2) & jnp.logical_not(turn))(ret(m, c).start)
        else:
            pl.when(me >= 2 * m)(ret(m, c).start)

    def send_back_far(m, c):
        if m == 2:
            pl.when(jnp.logical_not(turn_mate))(functools.partial(send_back, m, c))
        else:
            send_back(m, c)

    order = ((2, 0), (2, 1), (1, 0), (4, 0), (1, 1), (3, 0), (4, 1), (3, 1))
    after = {
        0: (((1, 0),), ()),
        1: (((4, 0),), ((2, 0),)),
        2: (((1, 1),), ((2, 1),)),
        3: (((3, 0), (4, 1)), ((1, 0),)),
        4: ((), ((4, 0),)),
        5: (((3, 1),), ((1, 1),)),
        6: ((), ((3, 0),)),
        7: ((), ((4, 1),)),
    }

    arrived(2, 0)
    arrived(2, 1)

    def body(step, carry):
        m, c = jnp.int32(0), jnp.int32(0)
        for i, (far, part) in enumerate(order):
            here = (step == i).astype(jnp.int32)
            m += far * here
            c += part * here
        slot = lax.rem(m - 1 + odd, hops)
        to_sib(slot + odd, c).wait_recv()
        far_blocks(m, slot, c)
        part_to_sib(slot, c).start()

        for i, (fresh, done) in after.items():

            @pl.when(step == i)
            def _():
                for pair in done:
                    send_back_far(*pair)
                for pair in fresh:
                    arrived(*pair)

        return carry

    lax.fori_loop(0, len(order), body, 0)

    out_query_ref[...] = (acc[...] * factor).astype(BF16)
    send_back(3, 1)

    @pl.when(turn_mate)
    def _():
        for c in (0, 1):
            send_back(2, c)

    @pl.when(odd == 0)
    def _():
        for c in (0, 1):
            part_to_sib(0, c).wait_recv()
            own_part[:, parts[c]] += sib_part[0, c] * row_last[:, c * half : c * half + half]

    for m in (2, 1, 4, 3):
        for c in (0, 1):

            @pl.when(returns(m))
            def _():
                ret(m, c).wait_recv()
                own_part[:, parts[c]] += (
                    ret_in[m - 1, c].astype(F32) * row_last[:, c * half : c * half + half]
                )

    out_key_ref[...] = (own_part[pl.ds(0, dh)] * factor).T.astype(BF16)
    out_value_ref[...] = own_part[pl.ds(dh, dh)].T.astype(BF16)

    for c in (0, 1):
        for m in (1, 2):
            pl.when(sends(m, c))(fwd(m, c).wait_send)
            pl.when(relays(m))(relay(m, c).wait_send)
        if c == 0:
            pl.when(turn_mate)(cross(c).wait_send)
        pl.when(turn)(aside(c).wait_send)
        pl.when((me >= 2) & jnp.logical_not(turn))(ret(1, c).wait_send)
        for m in range(2, hops + 1):
            pl.when(me >= 2 * m)(ret(m, c).wait_send)
        for slot in range(hops):
            part_to_sib(slot, c).wait_send()
            to_sib(slot + odd, c).wait_send()


def hand_on(q_in, k_in, v_in, q_out, k_out, v_out, sem):
    copies = [
        pltpu.make_async_copy(src, dst, sem.at[i])
        for i, (src, dst) in enumerate(((q_in, q_out), (k_in, k_out), (v_in, v_out)))
    ]
    for copy in copies:
        copy.start()
    for copy in copies:
        copy.wait()


def solution(mesh):
    seq, fold = mesh.shape["seq"], mesh.shape["fold"]

    def body(query, keys, values, grad_out, head_bias, doc_ids):
        rows, dh = keys.shape
        heads = query.shape[1] // dh
        hops = MAXDOC // rows // 2
        wide = heads * dh
        block = rows + 16
        vmem = pl.BlockSpec(memory_space=pltpu.VMEM)
        hbm = pl.BlockSpec(memory_space=pl.ANY)
        dma = pltpu.SemaphoreType.DMA
        shapes = (
            jax.ShapeDtypeStruct((rows, wide), BF16),
            jax.ShapeDtypeStruct((rows, dh), BF16),
            jax.ShapeDtypeStruct((rows, dh), BF16),
        )
        grads = pl.pallas_call(
            functools.partial(kernel, seq, fold, rows, dh, heads),
            out_shape=tuple(pltpu.VMEM(x.shape, x.dtype) for x in shapes),
            in_specs=[pl.BlockSpec(memory_space=pltpu.SMEM), vmem, hbm, hbm, hbm, hbm],
            out_specs=(vmem, vmem, vmem),
            scratch_shapes=[
                pltpu.VMEM((rows, wide), BF16),
                pltpu.VMEM((wide, rows), BF16),
                pltpu.VMEM((rows, wide), BF16),
                pltpu.VMEM((wide, rows), BF16),
                pltpu.VMEM((rows, wide), BF16),
                pltpu.VMEM((wide, rows), BF16),
                pltpu.VMEM((rows, dh), BF16),
                pltpu.VMEM((hops + 1, 2, block, dh), BF16),
                pltpu.VMEM((hops, 2, block, dh), BF16),
                pltpu.VMEM((rows, wide), F32),
                pltpu.VMEM((2 * dh, rows), F32),
                pltpu.VMEM((hops, 2, 2 * dh, rows // 2), F32),
                pltpu.VMEM((hops, 2, 2 * dh, rows // 2), F32),
                pltpu.VMEM((hops, 2, 2 * dh, rows // 2), F32),
                pltpu.VMEM((hops, 2, 2 * dh, rows // 2), BF16),
                pltpu.VMEM((hops, 2, 2 * dh, rows // 2), BF16),
                pltpu.VMEM((2, 2 * dh, rows // 2), BF16),
                dma((5,)),
                dma((2 * hops + 2,)), dma((2 * hops,)),
                dma((2 * hops,)), dma((2 * hops,)),
                dma((2 * hops,)), dma((2 * hops,)),
                dma((2 * hops,)), dma((2 * hops,)),
                dma((2,)), dma((2,)),
            ],
            compiler_params=pltpu.CompilerParams(
                collective_id=0, has_side_effects=True, vmem_limit_bytes=58 << 20
            ),
        )(head_bias, doc_ids, query, keys, values, grad_out)
        return pl.pallas_call(
            hand_on,
            out_shape=shapes,
            in_specs=[vmem] * 3,
            out_specs=(hbm,) * 3,
            scratch_shapes=[dma((3,))],
            compiler_params=pltpu.CompilerParams(vmem_limit_bytes=1 << 20),
        )(*grads)

    split = P(("seq", "fold"), None)
    return jax.shard_map(
        body,
        mesh=mesh,
        in_specs=(split, split, split, split, P(), P(("seq", "fold"))),
        out_specs=(split, split, split),
        check_vma=False,
    )
```

time: 47 us -> 44.2 us (0.940)
  Pallas kernels: 46.2 us -> 43.4 us
    pallas_call x1, Pallas kernels: 45.4 us -> 42.6 us  [body(): pl.pallas_call(functools.partial(kernel, seq, fold, rows, dh, heads), out...]
where the time goes in v2:
time: 44.2 us; the launch traced here: 44.1 us
  Pallas kernels  43.4 us (98%)
  between operations  0.64 us (1%)
    pallas_call x1, Pallas kernels, body(): pl.pallas_call(functools.partial(kernel, seq, fold, rows, dh, heads), out...  42.6 us

profile of v2, /device:TPU:222, one launch (start us, length us, event | category | flops | bytes accessed | tf_op | source)
XLA Modules:
  0.0 44.1 jit_solution(11490595248552948231)
XLA Ops:
  0.6 42.6 %shard_map.85 = (bf16[256,1024]{1,0:T(8,128)(2,1)S(1)}, bf16[256,128]{1,0:T(8,128)(2,1)S(1)}, bf16[256,128]{1,0:T(8,128)(2,1)S(1)}) custom-call(f32[8]{0:T(128)} %bias_ref.1, s32[256]{0:T(256)} %ids_ref.1, bf16[256,1024]{1,0:T(8,128)(2,1)} %query_ref.1, bf16[256,128]{1,0:T(8,128)(2,1)} %keys_ref.1, bf16[256,128]{1,0:T(8,128)(2,1)} %values_ref.1, ...), custom_call_target="tpu_custom_call" | custom-call | tf_op jit(solution)/shard_map/pallas_call | solution.py:377
  43.2 0.9 %shard_map.86 = (bf16[256,1024]{1,0:T(8,128)(2,1)}, bf16[256,128]{1,0:T(8,128)(2,1)}, bf16[256,128]{1,0:T(8,128)(2,1)}) custom-call(bf16[256,1024]{1,0:T(8,128)(2,1)S(1)} %get-tuple-element.6.q_in, bf16[256,128]{1,0:T(8,128)(2,1)S(1)} %get-tuple-element.7.k_in, bf16[256,128]{1,0:T(8,128)(2,1)S(1)} %get-tuple-element.8.v_in), custom_call_target="tpu_custom_call" | custom-call | tf_op jit(solution)/shard_map/pallas_call | solution.py:411

commit v3 on v2

--- a/solution.py
+++ b/solution.py
@@ -25,11 +25,11 @@
 
 def kernel(
     seq, fold, rows, dh, heads,
-    bias_ref, ids_ref, query_ref, keys_ref, values_ref, grad_ref,
+    bias_hbm, ids_hbm, query_ref, keys_ref, values_ref, grad_ref,
     out_query_ref, out_key_ref, out_value_ref,
     q_nat, q_tra, do_nat, do_tra, dom_nat, dom_tra, v_own,
     blocks, sib_blocks, acc, own_part, part_d, part_o, sib_part, ret_out, ret_in, aside_in,
-    load_sem, fwd_send, fwd_recv, sib_send, sib_recv, sibp_send, sibp_recv, ret_send, ret_recv,
+    bias_ref, ids_ref, load_sem, fwd_send, fwd_recv, sib_send, sib_recv, sibp_send, sibp_recv, ret_send, ret_recv,
     aside_send, aside_recv,
 ):
     peers = seq * fold
@@ -52,21 +52,6 @@
     turn_mate = turns(me - 2)
     turn_ahead = turns(me + 2)
 
-    barrier = pltpu.get_barrier_semaphore()
-    partners = jnp.int32(1)
-    for hop in range(1, hops + 1):
-        for far in (2 * hop, -2 * hop):
-            valid = (me + far >= 0) & (me + far < peers)
-            partners += valid.astype(jnp.int32)
-
-            @pl.when(valid)
-            def _():
-                pl.semaphore_signal(
-                    barrier, inc=1, device_id=device(me + far), device_id_type=MESH
-                )
-
-    pl.semaphore_signal(barrier, inc=1, device_id=sibling, device_id_type=MESH)
-
     cols = [pl.ds(h * dh, dh) for h in range(heads)]
     parts = [pl.ds(c * half, half) for c in (0, 1)]
     k_rows, v_rows, id_rows = pl.ds(0, half), pl.ds(half, half), pl.ds(rows, 16)
@@ -74,11 +59,30 @@
         pltpu.make_async_copy(keys_ref.at[parts[0]], blocks.at[0, 0, k_rows], load_sem.at[0]),
         pltpu.make_async_copy(keys_ref.at[parts[1]], blocks.at[0, 1, k_rows], load_sem.at[1]),
         pltpu.make_async_copy(values_ref, v_own, load_sem.at[2]),
-        pltpu.make_async_copy(query_ref, q_nat, load_sem.at[3]),
-        pltpu.make_async_copy(grad_ref, do_nat, load_sem.at[4]),
+        pltpu.make_async_copy(ids_hbm, ids_ref, load_sem.at[3]),
+        pltpu.make_async_copy(bias_hbm, bias_ref, load_sem.at[4]),
+        pltpu.make_async_copy(query_ref, q_nat, load_sem.at[5]),
+        pltpu.make_async_copy(grad_ref, do_nat, load_sem.at[6]),
     ]
     for load in loads:
         load.start()
+
+    barrier = pltpu.get_barrier_semaphore()
+    partners = jnp.int32(1)
+    for hop in range(1, hops + 1):
+        for far in (2 * hop, -2 * hop):
+            valid = (me + far >= 0) & (me + far < peers)
+            partners += valid.astype(jnp.int32)
+
+            @pl.when(valid)
+            def _():
+                pl.semaphore_signal(
+                    barrier, inc=1, device_id=device(me + far), device_id_type=MESH
+                )
+
+    pl.semaphore_signal(barrier, inc=1, device_id=sibling, device_id_type=MESH)
+
+    loads[3].wait()
 
     ids_row = ids_ref[...].astype(F32).reshape(1, rows)
     first = ids_row[:, 0:1]
@@ -112,8 +116,8 @@
             return (me + 2 < peers) & jnp.logical_not(turn_ahead)
         return me + 2 * m < peers
 
-    def returns(m):
-        if m == 1:
+    def returns(m, c):
+        if m == 1 and c == 1:
             return (me + 2 < peers) & jnp.logical_not(turn_ahead)
         return me + 2 * m < peers
 
@@ -163,7 +167,7 @@
         for c in (0, 1):
             to_sib(0, c).start()
 
-    for load in loads[3:]:
+    for load in loads[4:]:
         load.wait()
     for h in range(heads):
         q_tra[cols[h], :] = q_nat[:, cols[h]].T
@@ -244,7 +248,7 @@
         def _():
             ret_out[m - 1, c] = part_d[m - 1, c].astype(BF16)
 
-        if m == 2:
+        if m == 2 and c == 1:
 
             @pl.when(turn_mate)
             def _():
@@ -253,28 +257,28 @@
                     ret_out[1, c].astype(F32) + aside_in[c].astype(F32)
                 ).astype(BF16)
 
-        if m == 1:
+        if m == 1 and c == 1:
             pl.when(turn)(aside(c).start)
             pl.when((me >= 2) & jnp.logical_not(turn))(ret(m, c).start)
         else:
             pl.when(me >= 2 * m)(ret(m, c).start)
 
     def send_back_far(m, c):
-        if m == 2:
+        if m == 2 and c == 1:
             pl.when(jnp.logical_not(turn_mate))(functools.partial(send_back, m, c))
         else:
             send_back(m, c)
 
-    order = ((2, 0), (2, 1), (1, 0), (4, 0), (1, 1), (3, 0), (4, 1), (3, 1))
+    order = ((2, 0), (2, 1), (1, 0), (4, 0), (1, 1), (3, 0), (3, 1), (4, 1))
     after = {
         0: (((1, 0),), ()),
         1: (((4, 0),), ((2, 0),)),
         2: (((1, 1),), ((2, 1),)),
-        3: (((3, 0), (4, 1)), ((1, 0),)),
-        4: ((), ((4, 0),)),
+        3: (((3, 0),), ((1, 0),)),
+        4: (((4, 1),), ((4, 0),)),
         5: (((3, 1),), ((1, 1),)),
         6: ((), ((3, 0),)),
-        7: ((), ((4, 1),)),
+        7: ((), ((3, 1),)),
     }
 
     arrived(2, 0)
@@ -305,12 +309,11 @@
     lax.fori_loop(0, len(order), body, 0)
 
     out_query_ref[...] = (acc[...] * factor).astype(BF16)
-    send_back(3, 1)
+    send_back(4, 1)
 
     @pl.when(turn_mate)
     def _():
-        for c in (0, 1):
-            send_back(2, c)
+        send_back(2, 1)
 
     @pl.when(odd == 0)
     def _():
@@ -318,18 +321,21 @@
             part_to_sib(0, c).wait_recv()
             own_part[:, parts[c]] += sib_part[0, c] * row_last[:, c * half : c * half + half]
 
-    for m in (2, 1, 4, 3):
+    def add_back(m, c):
+        @pl.when(returns(m, c))
+        def _():
+            ret(m, c).wait_recv()
+            own_part[:, parts[c]] += (
+                ret_in[m - 1, c].astype(F32) * row_last[:, c * half : c * half + half]
+            )
+
+    for m in (2, 1, 4):
         for c in (0, 1):
-
-            @pl.when(returns(m))
-            def _():
-                ret(m, c).wait_recv()
-                own_part[:, parts[c]] += (
-                    ret_in[m - 1, c].astype(F32) * row_last[:, c * half : c * half + half]
-                )
-
-    out_key_ref[...] = (own_part[pl.ds(0, dh)] * factor).T.astype(BF16)
-    out_value_ref[...] = own_part[pl.ds(dh, dh)].T.astype(BF16)
+            add_back(m, c)
+    for c in (0, 1):
+        add_back(3, c)
+        out_key_ref[parts[c]] = (own_part[pl.ds(0, dh), parts[c]] * factor).T.astype(BF16)
+        out_value_ref[parts[c]] = own_part[pl.ds(dh, dh), parts[c]].T.astype(BF16)
 
     for c in (0, 1):
         for m in (1, 2):
@@ -337,8 +343,11 @@
             pl.when(relays(m))(relay(m, c).wait_send)
         if c == 0:
             pl.when(turn_mate)(cross(c).wait_send)
-        pl.when(turn)(aside(c).wait_send)
-        pl.when((me >= 2) & jnp.logical_not(turn))(ret(1, c).wait_send)
+        if c == 1:
+            pl.when(turn)(aside(c).wait_send)
+            pl.when((me >= 2) & jnp.logical_not(turn))(ret(1, c).wait_send)
+        else:
+            pl.when(me >= 2)(ret(1, c).wait_send)
         for m in range(2, hops + 1):
             pl.when(me >= 2 * m)(ret(m, c).wait_send)
         for slot in range(hops):
@@ -347,9 +356,11 @@
 
 
 def hand_on(q_in, k_in, v_in, q_out, k_out, v_out, sem):
+    size = q_in.shape[0] // 4
+    pairs = [(q_in.at[pl.ds(i * size, size)], q_out.at[pl.ds(i * size, size)]) for i in range(4)]
+    pairs += [(k_in, k_out), (v_in, v_out)]
     copies = [
-        pltpu.make_async_copy(src, dst, sem.at[i])
-        for i, (src, dst) in enumerate(((q_in, q_out), (k_in, k_out), (v_in, v_out)))
+        pltpu.make_async_copy(src, dst, sem.at[i]) for i, (src, dst) in enumerate(pairs)
     ]
     for copy in copies:
         copy.start()
@@ -377,7 +388,7 @@
         grads = pl.pallas_call(
             functools.partial(kernel, seq, fold, rows, dh, heads),
             out_shape=tuple(pltpu.VMEM(x.shape, x.dtype) for x in shapes),
-            in_specs=[pl.BlockSpec(memory_space=pltpu.SMEM), vmem, hbm, hbm, hbm, hbm],
+            in_specs=[hbm] * 6,
             out_specs=(vmem, vmem, vmem),
             scratch_shapes=[
                 pltpu.VMEM((rows, wide), BF16),
@@ -397,7 +408,9 @@
                 pltpu.VMEM((hops, 2, 2 * dh, rows // 2), BF16),
                 pltpu.VMEM((hops, 2, 2 * dh, rows // 2), BF16),
                 pltpu.VMEM((2, 2 * dh, rows // 2), BF16),
-                dma((5,)),
+                pltpu.SMEM((heads,), F32),
+                pltpu.VMEM((rows,), jnp.int32),
+                dma((7,)),
                 dma((2 * hops + 2,)), dma((2 * hops,)),
                 dma((2 * hops,)), dma((2 * hops,)),
                 dma((2 * hops,)), dma((2 * hops,)),
@@ -413,7 +426,7 @@
             out_shape=shapes,
             in_specs=[vmem] * 3,
             out_specs=(hbm,) * 3,
-            scratch_shapes=[dma((3,))],
+            scratch_shapes=[dma((6,))],
             compiler_params=pltpu.CompilerParams(vmem_limit_bytes=1 << 20),
         )(*grads)
 

time: 44.2 us -> 42.9 us (0.971)
  Pallas kernels: 43.4 us -> 41.8 us
    pallas_call x1, Pallas kernels: 42.6 us -> 40.9 us  [body(): pl.pallas_call(functools.partial(kernel, seq, fold, rows, dh, heads), out...]
where the time goes in v3:
time: 42.9 us; the launch traced here: 42.5 us
  Pallas kernels  41.8 us (97%)
  between operations  0.64 us (1%)
    pallas_call x1, Pallas kernels, body(): pl.pallas_call(functools.partial(kernel, seq, fold, rows, dh, heads), out...  40.9 us
    pallas_call x1, Pallas kernels, body(): pl.pallas_call(hand_on, out_shape=shapes, in_specs=[vmem] * 3, out_specs=...  0.88 us

profile of v3, /device:TPU:222, one launch (start us, length us, event | category | flops | bytes accessed | tf_op | source)
XLA Modules:
  0.0 42.5 jit_solution(2467364919152814235)
XLA Ops:
  0.6 40.9 %shard_map.85 = (bf16[256,1024]{1,0:T(8,128)(2,1)S(1)}, bf16[256,128]{1,0:T(8,128)(2,1)S(1)}, bf16[256,128]{1,0:T(8,128)(2,1)S(1)}) custom-call(f32[8]{0:T(128)} %bias_hbm.1, s32[256]{0:T(256)} %ids_hbm.1, bf16[256,1024]{1,0:T(8,128)(2,1)} %query_ref.1, bf16[256,128]{1,0:T(8,128)(2,1)} %keys_ref.1, bf16[256,128]{1,0:T(8,128)(2,1)} %values_ref.1, ...), custom_call_target="tpu_custom_call" | custom-call | tf_op jit(solution)/shard_map/pallas_call | solution.py:388
  41.6 0.9 %shard_map.86 = (bf16[256,1024]{1,0:T(8,128)(2,1)}, bf16[256,128]{1,0:T(8,128)(2,1)}, bf16[256,128]{1,0:T(8,128)(2,1)}) custom-call(bf16[256,1024]{1,0:T(8,128)(2,1)S(1)} %get-tuple-element.6.q_in, bf16[256,128]{1,0:T(8,128)(2,1)S(1)} %get-tuple-element.7.k_in, bf16[256,128]{1,0:T(8,128)(2,1)S(1)} %get-tuple-element.8.v_in), custom_call_target="tpu_custom_call" | custom-call | tf_op jit(solution)/shard_map/pallas_call | solution.py:424

commit v4 on v3

--- a/solution.py
+++ b/solution.py
@@ -87,12 +87,7 @@
     ids_row = ids_ref[...].astype(F32).reshape(1, rows)
     first = ids_row[:, 0:1]
     last = ids_row[:, rows - 1 : rows]
-    ids_u = jnp.broadcast_to(ids_row, (rows, rows))
-    ids_t = ids_u.T
-    col_first = (ids_t[:, :dh] == first).astype(BF16)
-    col_last = (ids_t[:, :dh] == last).astype(BF16)
-    row_first = (ids_row == first).astype(BF16)
-    row_last = (ids_row == last).astype(F32)
+    col_last = (jnp.broadcast_to(ids_row, (dh, rows)).T == last).astype(BF16)
 
     def push(src, dst, c, far, extra=0):
         slot = 2 * (dst - 1) + c
@@ -167,6 +162,11 @@
         for c in (0, 1):
             to_sib(0, c).start()
 
+    ids_u = jnp.broadcast_to(ids_row, (rows, rows))
+    ids_t = ids_u.T
+    col_first = (ids_t[:, :dh] == first).astype(BF16)
+    row_first = (ids_row == first).astype(BF16)
+    row_last = (ids_row == last).astype(F32)
     for load in loads[4:]:
         load.wait()
     for h in range(heads):

time: 42.9 us -> 42.9 us (level)
  no operation moved by 1% of the time
where the time goes in v4:
time: 42.9 us; the launch traced here: 42.5 us
  Pallas kernels  41.8 us (97%)
  between operations  0.64 us (1%)
    pallas_call x1, Pallas kernels, body(): pl.pallas_call(functools.partial(kernel, seq, fold, rows, dh, heads), out...  40.9 us
    pallas_call x1, Pallas kernels, body(): pl.pallas_call(hand_on, out_shape=shapes, in_specs=[vmem] * 3, out_specs=...  0.88 us

profile of v4, /device:TPU:222, one launch (start us, length us, event | category | flops | bytes accessed | tf_op | source)
XLA Modules:
  0.0 42.5 jit_solution(16943730078941844501)
XLA Ops:
  0.6 40.9 %shard_map.85 = (bf16[256,1024]{1,0:T(8,128)(2,1)S(1)}, bf16[256,128]{1,0:T(8,128)(2,1)S(1)}, bf16[256,128]{1,0:T(8,128)(2,1)S(1)}) custom-call(f32[8]{0:T(128)} %bias_hbm.1, s32[256]{0:T(256)} %ids_hbm.1, bf16[256,1024]{1,0:T(8,128)(2,1)} %query_ref.1, bf16[256,128]{1,0:T(8,128)(2,1)} %keys_ref.1, bf16[256,128]{1,0:T(8,128)(2,1)} %values_ref.1, ...), custom_call_target="tpu_custom_call" | custom-call | tf_op jit(solution)/shard_map/pallas_call | solution.py:388
  41.6 0.9 %shard_map.86 = (bf16[256,1024]{1,0:T(8,128)(2,1)}, bf16[256,128]{1,0:T(8,128)(2,1)}, bf16[256,128]{1,0:T(8,128)(2,1)}) custom-call(bf16[256,1024]{1,0:T(8,128)(2,1)S(1)} %get-tuple-element.6.q_in, bf16[256,128]{1,0:T(8,128)(2,1)S(1)} %get-tuple-element.7.k_in, bf16[256,128]{1,0:T(8,128)(2,1)S(1)} %get-tuple-element.8.v_in), custom_call_target="tpu_custom_call" | custom-call | tf_op jit(solution)/shard_map/pallas_call | solution.py:424

commit v5 on v4

--- a/solution.py
+++ b/solution.py
@@ -356,8 +356,8 @@
 
 
 def hand_on(q_in, k_in, v_in, q_out, k_out, v_out, sem):
-    size = q_in.shape[0] // 4
-    pairs = [(q_in.at[pl.ds(i * size, size)], q_out.at[pl.ds(i * size, size)]) for i in range(4)]
+    size = q_in.shape[0] // 8
+    pairs = [(q_in.at[pl.ds(i * size, size)], q_out.at[pl.ds(i * size, size)]) for i in range(8)]
     pairs += [(k_in, k_out), (v_in, v_out)]
     copies = [
         pltpu.make_async_copy(src, dst, sem.at[i]) for i, (src, dst) in enumerate(pairs)
@@ -426,7 +426,7 @@
             out_shape=shapes,
             in_specs=[vmem] * 3,
             out_specs=(hbm,) * 3,
-            scratch_shapes=[dma((6,))],
+            scratch_shapes=[dma((10,))],
             compiler_params=pltpu.CompilerParams(vmem_limit_bytes=1 << 20),
         )(*grads)
 

time: 42.9 us -> 42.9 us (level)
  no operation moved by 1% of the time
where the time goes in v5:
time: 42.9 us; the launch traced here: 42.5 us
  Pallas kernels  41.8 us (97%)
  between operations  0.64 us (1%)
    pallas_call x1, Pallas kernels, body(): pl.pallas_call(functools.partial(kernel, seq, fold, rows, dh, heads), out...  40.9 us
    pallas_call x1, Pallas kernels, body(): pl.pallas_call(hand_on, out_shape=shapes, in_specs=[vmem] * 3, out_specs=...  0.91 us

profile of v5, /device:TPU:222, one launch (start us, length us, event | category | flops | bytes accessed | tf_op | source)
XLA Modules:
  0.0 42.5 jit_solution(14303612138351731007)
XLA Ops:
  0.6 40.9 %shard_map.85 = (bf16[256,1024]{1,0:T(8,128)(2,1)S(1)}, bf16[256,128]{1,0:T(8,128)(2,1)S(1)}, bf16[256,128]{1,0:T(8,128)(2,1)S(1)}) custom-call(f32[8]{0:T(128)} %bias_hbm.1, s32[256]{0:T(256)} %ids_hbm.1, bf16[256,1024]{1,0:T(8,128)(2,1)} %query_ref.1, bf16[256,128]{1,0:T(8,128)(2,1)} %keys_ref.1, bf16[256,128]{1,0:T(8,128)(2,1)} %values_ref.1, ...), custom_call_target="tpu_custom_call" | custom-call | tf_op jit(solution)/shard_map/pallas_call | solution.py:388
  41.6 0.9 %shard_map.86 = (bf16[256,1024]{1,0:T(8,128)(2,1)}, bf16[256,128]{1,0:T(8,128)(2,1)}, bf16[256,128]{1,0:T(8,128)(2,1)}) custom-call(bf16[256,1024]{1,0:T(8,128)(2,1)S(1)} %get-tuple-element.6.q_in, bf16[256,128]{1,0:T(8,128)(2,1)S(1)} %get-tuple-element.7.k_in, bf16[256,128]{1,0:T(8,128)(2,1)S(1)} %get-tuple-element.8.v_in), custom_call_target="tpu_custom_call" | custom-call | tf_op jit(solution)/shard_map/pallas_call | solution.py:424
